TPU v7x, 32 devices: a whole 2x2x4 slice. The times are simulated.
32 devices in a mesh: groups: 2 (over y), wide: 16 (over z, x, core).
Axes of the slice: x: 2, y: 2, z: 4, core: 2. Of those that a mesh axis runs over, the one named last changes fastest.
Arguments:
- points: float32 [64, 393216], P(None, ('groups', 'wide')), parts along dimension 1
- solution: float32 [32, 393216], P(None, ('groups', 'wide')), parts along dimension 1, may hold values from -6 to 6
- residual: float32 [32, 393216], P(None, ('groups', 'wide')), parts along dimension 1, may hold values from -6 to 6
- direction: float32 [32, 393216], P(None, ('groups', 'wide')), parts along dimension 1, may hold values from -6 to 6
- lengthscales: float32 [4], replicated, may hold values from 0.5 to 1
- noise_variance: float32 [4], replicated, may hold values from 0.1 to 1
- link_peer: int32 [32, 48, 2], P(('groups', 'wide')), parts along dimension 0, may hold values from 0 to 15, as said below
Outputs:
- new_solution: float32 [32, 393216], P(None, ('groups', 'wide')), parts along dimension 1
- new_residual: float32 [32, 393216], P(None, ('groups', 'wide')), parts along dimension 1
- new_direction: float32 [32, 393216], P(None, ('groups', 'wide')), parts along dimension 1
There are 2 independent parts, one for each index of `groups`. A program takes and returns all parts, laid end to end along the dimension named above; an argument that names none is the same for every part. Nothing has to cross between parts.
Inputs may be any that keep to these rules, and one draw needn't show every extreme that they name: `link_peer`: local block t of a device is linked with local block t of two other devices, named on side 0 and side 1: in a cyclic order of the devices drawn with the seed, they stand k places before and k places after it, with k = 1 + (t mod 7). What a device names on side 1 names it on side 0 for the same t. A device is linked with a given peer only through blocks t of one residue of t mod 7, hence through at most 7 blocks, and some pair of devices is linked through 7 blocks.
All inputs are finite; a program needn't handle non-finite values.
Results may differ from a plain program's by a relative error of at most 0.0003.
Values sent between devices are 32-bit elements; how exact they have to be, the bound alone decides.
A program may use at most 128 MiB of HBM per device.

v0:
```python
import jax
import jax.numpy as jnp
from jax import lax
from jax.sharding import PartitionSpec as P

highest = lax.Precision.HIGHEST


def kernel_tile(row_points, col_points, lengthscales):
    anchor = row_points[:, :, :1]
    row_shift = row_points - anchor
    col_shift = col_points - anchor
    row_norms = jnp.sum(row_shift * row_shift, axis=1)
    col_norms = jnp.sum(col_shift * col_shift, axis=1)
    inner_product = jnp.einsum("gda,gdb->gab", row_shift, col_shift, precision=highest)
    squared = row_norms[:, :, None] + col_norms[:, None, :] - 2.0 * inner_product
    distance = jnp.sqrt(jnp.maximum(squared, 0.0))
    scaled = distance[:, None, :, :] / lengthscales[None, :, None, None]
    support = jnp.maximum(1.0 - scaled, 0.0)
    return support**35 * (35.0 * scaled + 1.0)


def apply_ahead(kernel, vectors):
    return jnp.einsum("gsab,gsrb->gsra", kernel, vectors, precision=highest)


def apply_behind(kernel, vectors):
    return jnp.einsum("gsab,gsra->gsrb", kernel, vectors, precision=highest)


def on_device(points, solution, residual, direction, lengthscales, noise_variance, link_peer):
    devices = lax.axis_size("wide")
    my_index = lax.axis_index("wide")
    blocks = link_peer.shape[1]
    features = points.shape[0]
    block_points = points.shape[1] // blocks
    settings = lengthscales.shape[0]
    columns = direction.shape[0]
    probes = columns // settings
    rounds_count = min(blocks, devices // 2 - 1)
    slot_count = (blocks + rounds_count - 1) // rounds_count
    group_size = 4
    item_total = 2 * blocks
    block_coords = jnp.transpose(points.reshape(features, blocks, block_points), (1, 0, 2))
    block_vectors = jnp.transpose(
        direction.reshape(settings, probes, blocks, block_points), (2, 0, 1, 3)
    )
    item_peer = link_peer[0].reshape(-1)
    item_owned = (my_index < item_peer).astype(jnp.int32)
    item_block = jnp.arange(item_total, dtype=jnp.int32) // 2
    item_slot = item_block // rounds_count
    item_sent = 1 - item_owned
    target = jnp.where(item_sent == 1, item_peer, devices)
    outgoing_coords = (
        jnp.zeros((devices, slot_count, features, block_points), jnp.float32)
        .at[target, item_slot]
        .set(block_coords[item_block], mode="drop")
    )
    outgoing_vectors = (
        jnp.zeros((devices, slot_count, settings, probes, block_points), jnp.float32)
        .at[target, item_slot]
        .set(block_vectors[item_block], mode="drop")
    )
    incoming_coords, incoming_vectors = (
        lax.all_to_all(outgoing_coords, "wide", split_axis=0, concat_axis=0, tiled=True),
        lax.all_to_all(outgoing_vectors, "wide", split_axis=0, concat_axis=0, tiled=True),
    )

    def diagonal_turn(turn_index, running):
        first_block = turn_index * group_size
        own_points = lax.dynamic_slice_in_dim(block_coords, first_block, group_size, 0)
        own_vectors = lax.dynamic_slice_in_dim(block_vectors, first_block, group_size, 0)
        kernel = kernel_tile(own_points, own_points, lengthscales)
        return lax.dynamic_update_slice_in_dim(
            running, apply_ahead(kernel, own_vectors), first_block, 0
        )

    product = lax.fori_loop(0, blocks // group_size, diagonal_turn, jnp.zeros_like(block_vectors))
    item_order = jnp.argsort(1 - item_owned, stable=True)
    live_count = jnp.sum(item_owned)
    turn_count = (live_count + group_size - 1) // group_size
    returned = jnp.zeros((devices, slot_count, settings, probes, block_points), jnp.float32)

    def cross_turn(turn_index, state_pair):
        running, outgoing = state_pair
        position = turn_index * group_size + jnp.arange(group_size, dtype=jnp.int32)
        is_live = position < live_count
        chosen = item_order[jnp.minimum(position, item_total - 1)]
        own_block = item_block[chosen]
        peer_index = item_peer[chosen]
        slot_index = item_slot[chosen]
        weight = is_live.astype(jnp.float32)[:, None, None, None]
        own_points = block_coords[own_block]
        far_points = incoming_coords[peer_index, slot_index]
        own_vectors = block_vectors[own_block]
        far_vectors = incoming_vectors[peer_index, slot_index]
        kernel = kernel_tile(own_points, far_points, lengthscales)
        running = running.at[own_block].add(apply_ahead(kernel, far_vectors) * weight)
        destination = jnp.where(is_live, peer_index, devices)
        outgoing = outgoing.at[destination, slot_index].set(
            apply_behind(kernel, own_vectors), mode="drop"
        )
        return (running, outgoing)

    product, returned = lax.fori_loop(0, turn_count, cross_turn, (product, returned))
    arrived = lax.all_to_all(returned, "wide", split_axis=0, concat_axis=0, tiled=True)
    from_owners = (
        arrived[item_peer, item_slot] * (1 - item_owned).astype(jnp.float32)[:, None, None, None]
    )
    product = product + jnp.sum(
        from_owners.reshape(blocks, 2, settings, probes, block_points), axis=1
    )
    product_flat = jnp.transpose(product, (1, 2, 0, 3)).reshape(columns, blocks * block_points)
    noise_columns = jnp.repeat(noise_variance, probes)[:, None]
    image_field = noise_columns * direction + product_flat
    old_norm = lax.psum(jnp.sum(residual * residual, axis=1), "wide")
    curvature = lax.psum(jnp.sum(direction * image_field, axis=1), "wide")
    step_size = (old_norm / curvature)[:, None]
    new_residual = residual - step_size * image_field
    new_norm = lax.psum(jnp.sum(new_residual * new_residual, axis=1), "wide")
    new_solution = solution + step_size * direction
    new_direction = new_residual + (new_norm / old_norm)[:, None] * direction
    return (new_solution, new_residual, new_direction)


def solution(mesh):
    in_specs = (
        P(None, ("groups", "wide")),
        P(None, ("groups", "wide")),
        P(None, ("groups", "wide")),
        P(None, ("groups", "wide")),
        P(),
        P(),
        P(("groups", "wide"), None, None),
    )
    out_specs = (
        P(None, ("groups", "wide")),
        P(None, ("groups", "wide")),
        P(None, ("groups", "wide")),
    )
    return jax.shard_map(
        on_device, mesh=mesh, in_specs=in_specs, out_specs=out_specs, check_vma=False
    )
```

profile of v0, /device:TPU:0, one launch (start us, length us, event | category | flops | bytes accessed | tf_op | source)
XLA Modules:
  0.0 1189.8 jit_solution(7364773105965837455)
XLA Ops:
  8.5 15.2 %scatter_fusion.2 = f32[16,7,4,8,256]{4,3,2,1,0:T(8,128)} fusion(f32[16,7,4,8,256]{4,3,2,1,0:T(8,128)} %broadcast.427.clone, s32[96]{0:T(128)S(1)} %get-tuple-element.277, f32[96,4,8,256]{3,2,1,0:T(8,128)} %gather_fusion.8), kind=kCustom, calls=%fused_computation.13 | custom fusion | bytes 9437952 | tf_op jit(solution)/shard_map/scatter | solution.py:62
  23.7 7.9 all-to-all-start
  42.9 16.6 %scatter_fusion.3 = f32[16,7,64,256]{3,2,1,0:T(8,128)} fusion(f32[16,7,64,256]{3,2,1,0:T(8,128)} %broadcast_in_dim.26, s32[96]{0:T(128)S(1)} %get-tuple-element.277, f32[96,64,256]{2,1,0:T(8,128)} %gather_fusion.9), kind=kCustom, calls=%fused_computation.14 | custom fusion | bytes 18875136 | tf_op jit(solution)/shard_map/scatter | solution.py:57
  62.1 38.1 %all-to-all-done = f32[16,7,4,8,256]{4,3,2,1,0:T(8,128)} async-done(((f32[16,7,4,8,256]{4,3,2,1,0:T(8,128)}), f32[16,7,4,8,256]{4,3,2,1,0:T(8,128)}, u32[]{:S(2)}, u32[]{:S(2)}) %all-to-all-start) | async-done | bytes 3670048 | tf_op jit(solution)/shard_map/all_to_all | solution.py:66
  100.1 17.6 %all-to-all-start.1 = ((f32[16,7,64,256]{3,2,1,0:T(8,128)}), f32[16,7,64,256]{3,2,1,0:T(8,128)}, u32[]{:S(2)}, u32[]{:S(2)}) async-start(f32[16,7,64,256]{3,2,1,0:T(8,128)} %scatter_fusion.3), calls=%async_computation.1 | async-start | bytes 14680064 | tf_op jit(solution)/shard_map/all_to_all | solution.py:65
  119.1 100.4 %while.26 = (s32[]{:T(128)}, f32[48,4,8,256]{3,2,1,0:T(8,128)}, f32[48,4,8,256]{3,2,1,0:T(8,128)}, f32[48,64,256]{2,1,0:T(8,128)S(1)}, f32[4]{0:T(128)S(1)}, /*index=5*/s32[]{:T(128)}, s32[]{:T(128)}, s32[]{:T(128)}, s32[]{:T(128)}) while((s32[]{:T(128)}, f32[48,4,8,256]{3,2,1,0:T(8,128)}, f32[48,4,8,256]{3,2,1,0:T(8,128)}, ...), condition=%wide.region_4.5_spmd, body=%wide.region_2.4_spmd.sunk | while | flops 316931072 | bytes 2902183 | solution.py:78
  120.8 6.6 fusion.100
  129.2 6.6 fusion.100
  137.6 6.6 fusion.100
  145.9 6.6 fusion.100
  154.3 6.6 fusion.100
  162.7 6.6 fusion.100
  171.0 6.6 fusion.100
  179.4 6.6 fusion.100
  187.8 6.6 fusion.100
  196.1 6.6 fusion.100
  204.5 6.6 fusion.100
  212.9 6.6 fusion.100
  219.4 30.7 %all-to-all-done.1 = f32[16,7,64,256]{3,2,1,0:T(8,128)} async-done(((f32[16,7,64,256]{3,2,1,0:T(8,128)}), f32[16,7,64,256]{3,2,1,0:T(8,128)}, u32[]{:S(2)}, u32[]{:S(2)}) %all-to-all-start.1) | async-done | bytes 7340064 | tf_op jit(solution)/shard_map/all_to_all | solution.py:65
  252.5 775.4 %while.27 = (s32[]{:T(128)}, f32[48,4,8,256]{3,2,1,0:T(8,128)}, f32[16,7,4,8,256]{4,3,2,1,0:T(8,128)}, s32[]{:T(128)}, s32[96]{0:T(128)S(1)}, /*index=5*/s32[96]...) while((s32[]{:T(128)}, f32[48,4,8,256]{3,2,1,0:T(8,128)}, ...), condition=%wide.region_14.15_spmd.clone, body=%wide.region_9.14_spmd.clone.sunk | while | flops 431558048 | bytes 36472392 | solution.py:105
  276.3 6.4 fusion.112
  308.7 6.4 fusion.112
  341.0 6.4 fusion.112
  373.3 6.4 fusion.112
  405.6 6.4 fusion.112
  437.9 6.4 fusion.112
  470.2 6.4 fusion.112
  502.5 6.4 fusion.112
  534.8 6.4 fusion.112
  567.1 6.4 fusion.112
  599.4 6.4 fusion.112
  631.7 6.4 fusion.112
  664.0 6.4 fusion.112
  696.3 6.4 fusion.112
  728.7 6.4 fusion.112
  761.0 6.4 fusion.112
  793.3 6.4 fusion.112
  825.6 6.4 fusion.112
  857.9 6.4 fusion.112
  890.2 6.4 fusion.112
  922.5 6.4 fusion.112
  954.8 6.4 fusion.112
  987.1 6.4 fusion.112
  1019.4 6.4 fusion.112
  1027.9 4.6 all-to-all-start.2
  1032.8 68.2 %all-to-all-done.2 = f32[16,7,4,8,256]{4,3,2,1,0:T(8,128)} async-done(((f32[16,7,4,8,256]{4,3,2,1,0:T(8,128)}), f32[16,7,4,8,256]{4,3,2,1,0:T(8,128)}, u32[]{:S(2)}, u32[]{:S(2)}) %all-to-all-start.2) | async-done | bytes 3670048 | tf_op jit(solution)/shard_map/all_to_all | solution.py:106
  1107.9 45.5 %all-reduce = (f32[32]{0:T(128)S(1)}, f32[32]{0:T(128)S(1)}) all-reduce(f32[32]{0:T(128)S(1)} %get-tuple-element.279, f32[32]{0:T(128)S(1)} %get-tuple-element.278), channel_id=1, replica_groups=mesh['groups'=2,'wide'=16] {'wide'}, use_global_device_ids=true, to_apply=%region_1.2 | all-reduce | flops 64 | bytes 512 | tf_op jit(solution)/shard_map/psum | solution.py:116
  1157.5 29.5 %psum.23 = f32[32]{0:T(128)S(1)} all-reduce(f32[32]{0:T(128)S(1)} %get-tuple-element.269), channel_id=1, replica_groups=mesh['groups'=2,'wide'=16] {'wide'}, use_global_device_ids=true, to_apply=%region_19.20 | all-reduce | flops 32 | bytes 256 | tf_op jit(solution)/shard_map/psum | solution.py:120
  (801 shorter events, 679.2 us)
Async XLA Ops:
  23.7 76.4 %all-to-all-start = ((f32[16,7,4,8,256]{4,3,2,1,0:T(8,128)}), f32[16,7,4,8,256]{4,3,2,1,0:T(8,128)}, u32[]{:S(2)}, u32[]{:S(2)}) async-start(f32[16,7,4,8,256]{4,3,2,1,0:T(8,128)} %scatter_fusion.2), calls=%async_computation | async-start | bytes 7340032 | tf_op jit(solution)/shard_map/all_to_all | solution.py:66
  62.1 57.0 %copy-start.9 = (f32[4]{0:T(128)S(1)}, f32[4]{0:T(128)}, u32[]{:S(2)}) copy-start(f32[4]{0:T(128)} %param.15) | copy-start | bytes 52
  100.1 150.0 %all-to-all-start.1 = ((f32[16,7,64,256]{3,2,1,0:T(8,128)}), f32[16,7,64,256]{3,2,1,0:T(8,128)}, u32[]{:S(2)}, u32[]{:S(2)}) async-start(f32[16,7,64,256]{3,2,1,0:T(8,128)} %scatter_fusion.3), calls=%async_computation.1 | async-start | bytes 14680064 | tf_op jit(solution)/shard_map/all_to_all | solution.py:65
  264.8 6.3 copy-start.2
  276.3 8.5 copy-start.1
  297.1 6.3 copy-start.2
  308.6 8.5 copy-start.1
  329.4 6.3 copy-start.2
  340.9 8.5 copy-start.1
  361.7 6.3 copy-start.2
  373.3 8.5 copy-start.1
  394.0 6.3 copy-start.2
  405.6 8.5 copy-start.1
  426.4 6.3 copy-start.2
  437.9 8.5 copy-start.1
  458.7 6.3 copy-start.2
  470.2 8.5 copy-start.1
  491.0 6.3 copy-start.2
  502.5 8.5 copy-start.1
  523.3 6.3 copy-start.2
  534.8 8.5 copy-start.1
  555.6 6.3 copy-start.2
  567.1 8.5 copy-start.1
  587.9 6.3 copy-start.2
  599.4 8.5 copy-start.1
  620.2 6.3 copy-start.2
  631.7 8.5 copy-start.1
  652.5 6.3 copy-start.2
  664.0 8.5 copy-start.1
  684.8 6.3 copy-start.2
  696.3 8.5 copy-start.1
  717.1 6.3 copy-start.2
  728.6 8.5 copy-start.1
  749.4 6.3 copy-start.2
  761.0 8.5 copy-start.1
  781.7 6.3 copy-start.2
  793.3 8.5 copy-start.1
  814.0 6.3 copy-start.2
  825.6 8.5 copy-start.1
  846.4 6.3 copy-start.2
  857.9 8.5 copy-start.1
  878.7 6.3 copy-start.2
  890.2 8.5 copy-start.1
  922.5 8.5 copy-start.1
  954.8 8.5 copy-start.1
  987.1 8.5 copy-start.1
  1019.4 8.5 copy-start.1
  1027.9 73.1 %all-to-all-start.2 = ((f32[16,7,4,8,256]{4,3,2,1,0:T(8,128)}), f32[16,7,4,8,256]{4,3,2,1,0:T(8,128)}, u32[]{:S(2)}, u32[]{:S(2)}) async-start(f32[16,7,4,8,256]{4,3,2,1,0:T(8,128)} %get-tuple-element.175), calls=%async_computation.2 | async-start | bytes 7340032 | tf_op jit(solution)/shard_map/all_to_all | solution.py:106
  (34 other events, 84.3 us)
where the time goes:
time: 1200 us; the launch traced here: 1190 us
  local copies, waits for them, and re-layouts  464 us (39%)
  matrix products  381 us (32%)
  waiting for transfers between devices  137 us (11%)
  other arithmetic  99 us (8%)
  blocking collectives  75 us (6%)
  starting transfers between devices  30.1 us (3%)
    dot_general x36, matrix products, apply_ahead(): return jnp.einsum('gsab,gsrb->gsra', kernel, vectors, precision=highest)  233 us
    dot_general x24, matrix products, apply_behind(): return jnp.einsum('gsab,gsra->gsrb', kernel, vectors, precision=highest)  93.3 us
    gather x24, local copies, waits for them, and re-layouts, cross_turn(): far_points = incoming_coords[peer_index, slot_index]  87.6 us
    all_to_all x1, waiting for transfers between devices, on_device(): lax.all_to_all(returned, 'wide', split_axis=0, concat_axis=0, tiled=True)  68.2 us
    gather x24, local copies, waits for them, and re-layouts, cross_turn(): far_vectors = incoming_vectors[peer_index, slot_index]  62.2 us
    gather x24, local copies, waits for them, and re-layouts, cross_turn(): own_points = block_coords[own_block]  58.9 us
    gather x24, local copies, waits for them, and re-layouts, cross_turn(): own_vectors = block_vectors[own_block]  56.2 us
    dot_general x36, matrix products, kernel_tile(): jnp.einsum('gda,gdb->gab', row_shift, col_shift, precision=highest)  54.9 us
  transfers between devices with their start and end apart: 3, of which 3 were waited for; matrix products, arithmetic and copies ran while one was open for 11% of the time, Pallas kernels for 0%

commit v1 on v0

v1 whole, which is shorter than its diff:
```python
import functools

import jax
import jax.numpy as jnp
from jax import lax
from jax.experimental import pallas as pl
from jax.experimental.pallas import tpu as pltpu
from jax.sharding import PartitionSpec as P

VMEM = pltpu.VMEM
SMEM = pltpu.SMEM
VMEM_LIMIT = 56 * 1024 * 1024
SCALE = 35.0 ** (1.0 / 36.0)
TOP = 36.0 * SCALE / 35.0
ROW_CHUNK = 32


def split_three(x):
    first = x.astype(jnp.bfloat16)
    rest = x - first.astype(jnp.float32)
    second = rest.astype(jnp.bfloat16)
    third = (rest - second.astype(jnp.float32)).astype(jnp.bfloat16)
    return first, second, third


def norm_rows(norms, low):
    pieces = [piece.astype(jnp.float32) for piece in split_three(norms)]
    row = lax.broadcasted_iota(jnp.int32, (16, norms.shape[1]), 0)
    rows = jnp.where((row >= 3 - low) & (row < 6 - low), 1.0, 0.0)
    for index, piece in enumerate(pieces):
        rows = jnp.where(row == index + low, piece, rows)
    return rows.astype(jnp.bfloat16)


def squared_distances(row_shift, col_shift):
    row_norms = jnp.sum(row_shift * row_shift, axis=0, keepdims=True)
    col_norms = jnp.sum(col_shift * col_shift, axis=0, keepdims=True)
    r1, r2, r3 = split_three(row_shift)
    c1, c2, c3 = split_three(-2.0 * col_shift)
    left = jnp.concatenate([r1, r1, r2, r1, r3, r2, norm_rows(row_norms, 0)], axis=0)
    right = jnp.concatenate([c1, c2, c1, c3, c1, c2, norm_rows(col_norms, 3)], axis=0)
    return lax.dot_general(
        left, right, (((0,), (0,)), ((), ())), preferred_element_type=jnp.float32
    )


def split_vectors(vectors, setting, probes):
    rows = vectors[setting * probes : (setting + 1) * probes]
    high = rows.astype(jnp.bfloat16).astype(jnp.float32)
    return jnp.concatenate([high, rows - high], axis=0).astype(jnp.bfloat16)


def apply_tile(vectors, high, low, dim):
    dims = (((1,), (dim,)), ((), ()))
    both = lax.dot_general(vectors, high, dims, preferred_element_type=jnp.float32)
    both += lax.dot_general(vectors, low, dims, preferred_element_type=jnp.float32)
    half = both.shape[0] // 2
    return both[:half] + both[half:]


def tile_products(inverse_ref, row_shift, col_shift, row_vectors, col_vectors, dist_ref, high_ref, low_ref, probes):
    size = row_shift.shape[1]
    settings = high_ref.shape[0]
    floor = jnp.maximum(squared_distances(row_shift, col_shift), 1e-30)
    dist_ref[...] = floor * lax.rsqrt(floor)
    ahead, behind = [], []
    for setting in range(settings):
        inverse = inverse_ref[setting]
        for start in range(0, size, ROW_CHUNK):
            rows = pl.ds(start, ROW_CHUNK)
            w = jnp.maximum(SCALE - dist_ref[rows, :] * inverse, 0.0)
            w2 = w * w
            w4 = w2 * w2
            w8 = w4 * w4
            w16 = w8 * w8
            w32 = w16 * w16
            value = (w32 * (w2 * w)) * (TOP - w)
            high = value.astype(jnp.bfloat16)
            high_ref[setting, rows, :] = high
            low_ref[setting, rows, :] = (value - high.astype(jnp.float32)).astype(jnp.bfloat16)
        high, low = high_ref[setting], low_ref[setting]
        behind.append(apply_tile(split_vectors(row_vectors, setting, probes), high, low, 0))
        if col_vectors is not None:
            ahead.append(apply_tile(split_vectors(col_vectors, setting, probes), high, low, 1))
    behind = jnp.concatenate(behind, axis=0)
    return (jnp.concatenate(ahead, axis=0) if ahead else None), behind


def gather_kernel(size, index_ref, points_ref, direction_ref, out_ref, sem):
    features = points_ref.shape[0]
    columns = direction_ref.shape[0]

    def start(item, carry):
        block = pl.ds(pl.multiple_of(index_ref[item] * size, size), size)
        pltpu.make_async_copy(points_ref.at[:, block], out_ref.at[item, pl.ds(0, features)], sem).start()
        pltpu.make_async_copy(direction_ref.at[:, block], out_ref.at[item, pl.ds(features, columns)], sem).start()
        return carry

    lax.fori_loop(0, out_ref.shape[0], start, 0)
    pltpu.make_async_copy(out_ref, out_ref, sem).wait()


def gather_blocks(index, points, direction, size):
    rows = points.shape[0] + direction.shape[0]
    return pl.pallas_call(
        functools.partial(gather_kernel, size),
        out_shape=jax.ShapeDtypeStruct((index.shape[0], rows, size), jnp.float32),
        in_specs=[pl.BlockSpec(memory_space=SMEM)] + [pl.BlockSpec(memory_space=pl.ANY)] * 2,
        out_specs=pl.BlockSpec(memory_space=pl.ANY),
        scratch_shapes=[pltpu.SemaphoreType.DMA],
    )(index, points, direction)


def diagonal_kernel(size, probes, inverse_ref, points_ref, direction_ref, out_ref, dist_ref, high_ref, low_ref):
    def turn(block, carry):
        at = pl.ds(pl.multiple_of(block * size, size), size)
        own = points_ref[:, at]
        shift = own - own[:, 0:1]
        _, product = tile_products(
            inverse_ref, shift, shift, direction_ref[:, at], None, dist_ref, high_ref, low_ref, probes
        )
        out_ref[:, at] = product
        return carry

    lax.fori_loop(0, points_ref.shape[1] // size, turn, 0)


def tile_scratch(settings, size):
    return [
        pltpu.VMEM((size, size), jnp.float32),
        pltpu.VMEM((settings, size, size), jnp.bfloat16),
        pltpu.VMEM((settings, size, size), jnp.bfloat16),
    ]


def diagonal_products(inverse, points, direction, size):
    settings = inverse.shape[0]
    return pl.pallas_call(
        functools.partial(diagonal_kernel, size, direction.shape[0] // settings),
        out_shape=jax.ShapeDtypeStruct(direction.shape, jnp.float32),
        in_specs=[pl.BlockSpec(memory_space=SMEM)] + [pl.BlockSpec(memory_space=VMEM)] * 2,
        out_specs=pl.BlockSpec(memory_space=VMEM),
        scratch_shapes=tile_scratch(settings, size),
        compiler_params=pltpu.CompilerParams(vmem_limit_bytes=VMEM_LIMIT),
        cost_estimate=pl.CostEstimate(flops=40_000_000_000, bytes_accessed=6_000_000, transcendentals=0),
    )(inverse, points, direction)


def cross_kernel(size, probes, inverse_ref, index_ref, first_ref, points_ref, direction_ref, far_ref,
                 ahead_ref, behind_ref, dist_ref, high_ref, low_ref):
    item = pl.program_id(0)
    features = points_ref.shape[0]
    at = pl.ds(pl.multiple_of(index_ref[item] * size, size), size)
    own = points_ref[:, at]
    far = far_ref[0, 0:features, :]
    anchor = jnp.where(first_ref[item] == 1, own[:, 0:1], far[:, 0:1])
    ahead, behind = tile_products(
        inverse_ref, own - anchor, far - anchor, direction_ref[:, at], far_ref[0, features:, :],
        dist_ref, high_ref, low_ref, probes
    )
    ahead_ref[0] = ahead
    behind_ref[0] = behind


def cross_products(inverse, index, first, points, direction, far, size):
    settings = inverse.shape[0]
    items, rows = far.shape[:2]
    columns = direction.shape[0]
    result = jax.ShapeDtypeStruct((items, columns, size), jnp.float32)
    result_spec = pl.BlockSpec((1, columns, size), lambda i: (i, 0, 0))
    return pl.pallas_call(
        functools.partial(cross_kernel, size, columns // settings),
        grid=(items,),
        out_shape=(result, result),
        in_specs=[pl.BlockSpec(memory_space=SMEM)] * 3
        + [pl.BlockSpec(memory_space=VMEM)] * 2
        + [pl.BlockSpec((1, rows, size), lambda i: (i, 0, 0))],
        out_specs=(result_spec, result_spec),
        scratch_shapes=tile_scratch(settings, size),
        compiler_params=pltpu.CompilerParams(vmem_limit_bytes=VMEM_LIMIT),
    )(inverse, index, first, points, direction, far)


def combine_kernel(size, probes, noise_ref, own_ref, own_live_ref, sent_ref, sent_live_ref, ahead_ref, arrived_ref,
                   diagonal_ref, direction_ref, residual_ref, image_ref, sums_ref):
    settings = noise_ref.shape[0]
    for setting in range(settings):
        rows = pl.ds(setting * probes, probes)
        image_ref[rows, :] = diagonal_ref[rows, :] + noise_ref[setting] * direction_ref[rows, :]

    def add(item, carry):
        @pl.when(own_live_ref[item] == 1)
        def _():
            at = pl.ds(pl.multiple_of(own_ref[item] * size, size), size)
            image_ref[:, at] += ahead_ref[item]

        @pl.when(sent_live_ref[item] == 1)
        def _():
            at = pl.ds(pl.multiple_of(sent_ref[item] * size, size), size)
            image_ref[:, at] += arrived_ref[item]

        return carry

    lax.fori_loop(0, ahead_ref.shape[0], add, 0)

    def total(chunk, sums):
        at = pl.ds(pl.multiple_of(chunk * 128, 128), 128)
        r, d, m = residual_ref[:, at], direction_ref[:, at], image_ref[:, at]
        return (sums[0] + r * r, sums[1] + d * m, sums[2] + r * m, sums[3] + m * m)

    zero = jnp.zeros((direction_ref.shape[0], 128), jnp.float32)
    sums = lax.fori_loop(0, direction_ref.shape[1] // 128, total, (zero,) * 4)
    for index in range(4):
        sums_ref[index] = sums[index]


def combine(noise, own, own_live, sent, sent_live, ahead, arrived, diagonal, direction, residual, size):
    columns = direction.shape[0]
    return pl.pallas_call(
        functools.partial(combine_kernel, size, columns // noise.shape[0]),
        out_shape=(
            jax.ShapeDtypeStruct(direction.shape, jnp.float32),
            jax.ShapeDtypeStruct((4, columns, 128), jnp.float32),
        ),
        in_specs=[pl.BlockSpec(memory_space=SMEM)] * 5 + [pl.BlockSpec(memory_space=VMEM)] * 5,
        out_specs=(pl.BlockSpec(memory_space=VMEM),) * 2,
        compiler_params=pltpu.CompilerParams(vmem_limit_bytes=VMEM_LIMIT),
    )(noise, own, own_live, sent, sent_live, ahead, arrived, diagonal, direction, residual)


def slot_tables(link_peer, my_index, devices):
    blocks = link_peer.shape[1]
    rounds = min(blocks, devices // 2 - 1)
    slots = (blocks + rounds - 1) // rounds
    halves = (slots + 1) // 2
    peers = jnp.arange(devices, dtype=jnp.int32)
    match = (link_peer[0, :rounds, 0][None, :] == peers[:, None]) | (link_peer[0, :rounds, 1][None, :] == peers[:, None])
    linked = jnp.any(match, axis=1)
    residue = jnp.sum(jnp.where(match, jnp.arange(rounds, dtype=jnp.int32)[None, :], 0), axis=1)
    first = (my_index < peers) == ((my_index + peers) % 2 == 0)
    half = jnp.arange(halves, dtype=jnp.int32)[None, :]

    def table(offset):
        slot = 2 * half + offset[:, None]
        block = residue[:, None] + rounds * slot
        live = linked[:, None] & (block < blocks)
        return jnp.where(live, block, 0).reshape(-1), live.astype(jnp.int32).reshape(-1)

    own, own_live = table(jnp.where(first, 0, 1))
    sent, sent_live = table(jnp.where(first, 1, 0))
    lower = jnp.repeat((my_index < peers).astype(jnp.int32), halves)
    return own, own_live, sent, sent_live, lower


def on_device(points, solution, residual, direction, lengthscales, noise_variance, link_peer):
    devices = lax.axis_size("wide")
    my_index = lax.axis_index("wide")
    size = points.shape[1] // link_peer.shape[1]
    probes = direction.shape[0] // lengthscales.shape[0]
    inverse = SCALE / lengthscales
    own, own_live, sent, sent_live, lower = slot_tables(link_peer, my_index, devices)
    outgoing = gather_blocks(sent, points, direction, size)
    incoming = lax.all_to_all(outgoing, "wide", split_axis=0, concat_axis=0, tiled=True)
    diagonal = diagonal_products(inverse, points, direction, size)
    ahead, behind = cross_products(inverse, own, lower, points, direction, incoming, size)
    arrived = lax.all_to_all(behind, "wide", split_axis=0, concat_axis=0, tiled=True)
    image, sums = combine(
        noise_variance, own, own_live, sent, sent_live, ahead, arrived, diagonal, direction, residual, size
    )
    totals = lax.psum(jnp.sum(sums, axis=2), "wide")
    old_norm, curvature, mixed, square = totals[0], totals[1], totals[2], totals[3]
    step_size = old_norm / curvature
    new_norm = old_norm - 2.0 * step_size * mixed + step_size * step_size * square
    ratio = new_norm / old_norm
    new_residual = residual - step_size[:, None] * image
    new_solution = solution + step_size[:, None] * direction
    new_direction = new_residual + ratio[:, None] * direction
    return (new_solution, new_residual, new_direction)


def solution(mesh):
    split = P(None, ("groups", "wide"))
    in_specs = (split, split, split, split, P(), P(), P(("groups", "wide"), None, None))
    return jax.shard_map(
        on_device, mesh=mesh, in_specs=in_specs, out_specs=(split,) * 3, check_vma=False
    )
```

time: 1200 us -> 525 us (0.44)
  local copies, waits for them, and re-layouts: 464 us -> 3.14 us
  matrix products: 381 us -> 0 us
  Pallas kernels: 0 us -> 331 us
  other arithmetic: 99 us -> 7.25 us
  blocking collectives: 75 us -> 33.9 us
  waiting for transfers between devices: 137 us -> 113 us
    dot_general x96 -> x0, matrix products: 381 us -> none  [the longest x36 233 us: apply_ahead(): return jnp.einsum('gsab,gsrb->gsra', kernel, vectors, precision=highest)]
    gather x195 -> x0, local copies, waits for them, and re-layouts: 335 us -> none  [the longest x24 87.6 us: cross_turn(): far_points = incoming_coords[peer_index, slot_index]]
    pallas_call x0 -> x4, Pallas kernels: none -> 331 us  [the longest x1 192 us: gather_blocks(): pl.pallas_call(functools.partial(gather_kernel, size), out_shape=jax.Shap...]
    scatter x26 -> x0, local copies, waits for them, and re-layouts: 80.4 us -> none  [the longest x24 48.5 us: cross_turn(): outgoing.at[destination, slot_index]]
    scatter-add x24 -> x0, other arithmetic: 50.4 us -> none  [cross_turn(): running.at[own_block].add(apply_ahead(kernel, far_vectors) * weight)]
    psum x2 -> x1, blocking collectives: 75 us -> 33.9 us  [on_device(): totals = lax.psum(jnp.sum(sums, axis=2), 'wide')]
    while x144 -> x0, local copies, waits for them, and re-layouts: 26 us -> none
    all_to_all x3 -> x2, waiting for transfers between devices: 137 us -> 113 us  [the longest x1 113 us: on_device(): lax.all_to_all(outgoing, 'wide', split_axis=0, concat_axis=0, tiled=True)]
  transfers between devices with their start and end apart: 3 -> 2, of which waited for: 3 -> 1; matrix products, arithmetic and copies ran while one was open for 11% -> 0% of each run, Pallas kernels for 0% -> 10%
where the time goes in v1:
time: 525 us
  Pallas kernels  331 us (63%)
  waiting for transfers between devices  113 us (22%)
  starting transfers between devices  35.5 us (7%)
  blocking collectives  33.9 us (6%)
  other arithmetic  7.25 us (1%)
    pallas_call x1, Pallas kernels, gather_blocks(): pl.pallas_call(functools.partial(gather_kernel, size), out_shape=jax.Shap...  192 us
    all_to_all x1, waiting for transfers between devices, on_device(): lax.all_to_all(outgoing, 'wide', split_axis=0, concat_axis=0, tiled=True)  113 us
    pallas_call x1, Pallas kernels, cross_products(): pl.pallas_call(functools.partial(cross_kernel, size, columns // settings)...  77.7 us
    pallas_call x1, Pallas kernels, diagonal_products(): pl.pallas_call(functools.partial(diagonal_kernel, size, direction.shape[0...  53.1 us
    psum x1, blocking collectives, on_device(): totals = lax.psum(jnp.sum(sums, axis=2), 'wide')  33.9 us
    all_to_all x1, starting transfers between devices, on_device(): lax.all_to_all(behind, 'wide', split_axis=0, concat_axis=0, tiled=True)  28.1 us
  transfers between devices with their start and end apart: 2, of which 1 were waited for; matrix products, arithmetic and copies ran while one was open for 0% of the time, Pallas kernels for 10%

profile of v1, /device:TPU:0, one launch (start us, length us, event | category | flops | bytes accessed | tf_op | source)
XLA Modules:
  0.0 524.7 jit_solution(15016804145926117150)
XLA Ops:
  0.6 0.8 slice_bitcast_fusion.1
  1.4 0.1 select_reduce_fusion
  1.5 0.1 fusion.1
  1.6 0.1 multiply_add_fusion.2
  1.7 0.1 add.106
  1.8 0.1 and.38
  1.8 0.1 and.39
  1.9 0.1 add.102
  2.0 0.6 broadcast_select_fusion
  2.6 192.4 %shard_map.94 = f32[64,96,256]{2,1,0:T(8,128)} custom-call(s32[64]{0:T(128)} %get-tuple-element.22.index_ref.sent_ref, f32[64,12288]{1,0:T(8,128)} %points_ref.5, f32[32,12288]{1,0:T(8,128)} %direction_ref.7), custom_call_target="tpu_custom_call" | custom-call | tf_op jit(solution)/shard_map/pallas_call | solution.py:105
  195.0 0.0 copy-start.3
  195.0 7.4 %all-to-all-start = ((f32[64,96,256]{2,1,0:T(8,128)}), f32[64,96,256]{2,1,0:T(8,128)}, u32[]{:S(2)}, u32[]{:S(2)}) async-start(f32[64,96,256]{2,1,0:T(8,128)} %shard_map.94), calls=%async_computation | async-start | bytes 12582912 | tf_op jit(solution)/shard_map/all_to_all | solution.py:263
  202.4 0.1 broadcast_in_dim.42
  202.5 0.6 reshape.105.first_ref
  203.1 0.0 copy-done.3
  203.1 0.5 broadcast_divide_fusion.inverse_ref
  203.6 113.0 %all-to-all-done.far_ref = f32[64,96,256]{2,1,0:T(8,128)} async-done(((f32[64,96,256]{2,1,0:T(8,128)}), f32[64,96,256]{2,1,0:T(8,128)}, u32[]{:S(2)}, u32[]{:S(2)}) %all-to-all-start) | async-done | bytes 6291488 | tf_op jit(solution)/shard_map/all_to_all | solution.py:263
  316.6 77.7 %shard_map.95 = (f32[64,32,256]{2,1,0:T(8,128)}, f32[64,32,256]{2,1,0:T(8,128)}) custom-call(f32[4]{0:T(128)} %broadcast_divide_fusion.inverse_ref, s32[64]{0:T(128)} %get-tuple-element.23.index_ref.own_ref, s32[64]{0:T(128)} %reshape.105.first_ref, f32[64,12288]{1,0:T(8,128)} %points_ref.5, f32[32,12288]{1,0:T(8,128)} %direction_ref.7, ...), custom_call_target="tpu_custom_call" | custom-call | tf_op jit(solution)/shard_map/pallas_call | solution.py:171
  394.3 28.1 %all-to-all-start.1 = ((f32[64,32,256]{2,1,0:T(8,128)}), f32[64,32,256]{2,1,0:T(8,128)S(1)}, u32[]{:S(2)}, u32[]{:S(2)}) async-start(f32[64,32,256]{2,1,0:T(8,128)} %get-tuple-element.8), calls=%async_computation.1 | async-start | bytes 4194304 | tf_op jit(solution)/shard_map/all_to_all | solution.py:266
  422.4 0.5 fusion.7
  422.9 53.1 %shard_map.96.diagonal_ref = f32[32,12288]{1,0:T(8,128)} custom-call(f32[4]{0:T(128)} %broadcast_divide_fusion.inverse_ref, f32[64,12288]{1,0:T(8,128)} %points_ref.5, f32[32,12288]{1,0:T(8,128)} %direction_ref.7), custom_call_target="tpu_custom_call" | custom-call | flops 40000000000 | bytes 6000000 | tf_op jit(solution)/shard_map/pallas_call | solution.py:138
  475.9 0.0 all-to-all-done.1.arrived_ref
  476.0 0.0 copy-start.1
  476.0 1.3 copy-done.1
  477.3 0.0 copy-start
  477.3 0.0 copy-start.2
  477.3 8.1 %shard_map.97 = (f32[32,12288]{1,0:T(8,128)}, f32[4,32,128]{2,1,0:T(8,128)}) custom-call(f32[4]{0:T(128)} %noise_ref.1, s32[64]{0:T(128)} %get-tuple-element.23.index_ref.own_ref, s32[64]{0:T(128)} %get-tuple-element.21.own_live_ref, s32[64]{0:T(128)} %get-tuple-element.22.index_ref.sent_ref, s32[64]{0:T(128)} %get-tuple-element.20.sent_live_ref, ...), custom_call_target="tpu_custom_call" | custom-call | tf_op jit(solution)/shard_map/pallas_call | solution.py:219
  485.4 0.9 reduce_sum.19
  486.4 33.9 %psum.7 = f32[4,32]{1,0:T(4,128)S(1)} all-reduce(f32[4,32]{1,0:T(4,128)S(1)} %reduce_sum.19), channel_id=1, replica_groups=mesh['groups'=2,'wide'=16] {'wide'}, use_global_device_ids=true, to_apply=%region_3.4 | all-reduce | flops 128 | bytes 1024 | tf_op jit(solution)/shard_map/psum | solution.py:270
  520.3 0.0 copy-done
  520.3 0.0 copy-done.2
  520.3 4.4 multiply_add_fusion
  (4 shorter events, 0.0 us)
Async XLA Ops:
  195.0 8.1 %copy-start.3 = (f32[4]{0:T(128)S(1)}, f32[4]{0:T(128)}, u32[]{:S(2)}) copy-start(f32[4]{0:T(128)} %param.11) | copy-start | bytes 52
  195.0 121.6 %all-to-all-start = ((f32[64,96,256]{2,1,0:T(8,128)}), f32[64,96,256]{2,1,0:T(8,128)}, u32[]{:S(2)}, u32[]{:S(2)}) async-start(f32[64,96,256]{2,1,0:T(8,128)} %shard_map.94), calls=%async_computation | async-start | bytes 12582912 | tf_op jit(solution)/shard_map/all_to_all | solution.py:263
  394.3 81.7 %all-to-all-start.1 = ((f32[64,32,256]{2,1,0:T(8,128)}), f32[64,32,256]{2,1,0:T(8,128)S(1)}, u32[]{:S(2)}, u32[]{:S(2)}) async-start(f32[64,32,256]{2,1,0:T(8,128)} %get-tuple-element.8), calls=%async_computation.1 | async-start | bytes 4194304 | tf_op jit(solution)/shard_map/all_to_all | solution.py:266
  476.0 1.3 copy-start.1
  477.3 43.0 %copy-start = (f32[32,12288]{1,0:T(8,128)S(1)}, f32[32,12288]{1,0:T(8,128)}, u32[]{:S(2)}) copy-start(f32[32,12288]{1,0:T(8,128)} %direction_ref.7) | copy-start | bytes 4718596
  477.3 43.0 %copy-start.2 = (f32[32,12288]{1,0:T(8,128)S(1)}, f32[32,12288]{1,0:T(8,128)}, u32[]{:S(2)}) copy-start(f32[32,12288]{1,0:T(8,128)} %residual_ref.1) | copy-start | bytes 4718596

commit v2 on v1

--- a/solution.py
+++ b/solution.py
@@ -9,6 +9,7 @@
 
 VMEM = pltpu.VMEM
 SMEM = pltpu.SMEM
+MESH = pl.DeviceIdType.MESH
 VMEM_LIMIT = 56 * 1024 * 1024
 SCALE = 35.0 ** (1.0 / 36.0)
 TOP = 36.0 * SCALE / 35.0
@@ -86,43 +87,131 @@
     return (jnp.concatenate(ahead, axis=0) if ahead else None), behind
 
 
-def gather_kernel(size, index_ref, points_ref, direction_ref, out_ref, sem):
+def gather_kernel(size, sent_ref, own_ref, points_ref, direction_ref, out_ref, kept_ref):
     features = points_ref.shape[0]
-    columns = direction_ref.shape[0]
-
-    def start(item, carry):
-        block = pl.ds(pl.multiple_of(index_ref[item] * size, size), size)
-        pltpu.make_async_copy(points_ref.at[:, block], out_ref.at[item, pl.ds(0, features)], sem).start()
-        pltpu.make_async_copy(direction_ref.at[:, block], out_ref.at[item, pl.ds(features, columns)], sem).start()
-        return carry
-
-    lax.fori_loop(0, out_ref.shape[0], start, 0)
-    pltpu.make_async_copy(out_ref, out_ref, sem).wait()
-
-
-def gather_blocks(index, points, direction, size):
+
+    def copy(item, carry):
+        for index_ref, result_ref in ((sent_ref, out_ref), (own_ref, kept_ref)):
+            block = pl.ds(pl.multiple_of(index_ref[item] * size, size), size)
+            result_ref[item, 0:features, :] = points_ref[:, block]
+            result_ref[item, features:, :] = direction_ref[:, block]
+        return carry
+
+    lax.fori_loop(0, out_ref.shape[0], copy, 0)
+
+
+def gather_blocks(sent, own, points, direction, size):
     rows = points.shape[0] + direction.shape[0]
     return pl.pallas_call(
         functools.partial(gather_kernel, size),
-        out_shape=jax.ShapeDtypeStruct((index.shape[0], rows, size), jnp.float32),
-        in_specs=[pl.BlockSpec(memory_space=SMEM)] + [pl.BlockSpec(memory_space=pl.ANY)] * 2,
-        out_specs=pl.BlockSpec(memory_space=pl.ANY),
-        scratch_shapes=[pltpu.SemaphoreType.DMA],
-    )(index, points, direction)
-
-
-def diagonal_kernel(size, probes, inverse_ref, points_ref, direction_ref, out_ref, dist_ref, high_ref, low_ref):
-    def turn(block, carry):
+        out_shape=(jax.ShapeDtypeStruct((sent.shape[0], rows, size), jnp.float32),) * 2,
+        in_specs=[pl.BlockSpec(memory_space=SMEM)] * 2 + [pl.BlockSpec(memory_space=VMEM)] * 2,
+        out_specs=(pl.BlockSpec(memory_space=VMEM),) * 2,
+        compiler_params=pltpu.CompilerParams(vmem_limit_bytes=VMEM_LIMIT),
+    )(sent, own, points, direction)
+
+
+def greet(devices, me):
+    barrier = pltpu.get_barrier_semaphore()
+
+    def signal(step, carry):
+        pl.semaphore_signal(barrier, inc=1, device_id={"wide": (me + step) % devices}, device_id_type=MESH)
+        return carry
+
+    lax.fori_loop(1, devices, signal, 0)
+    pl.semaphore_wait(barrier, devices - 1)
+
+
+def exchange_kernel(devices, slots, size, probes, inverse_ref, points_ref, direction_ref, kept_ref, outgoing_ref,
+                    diagonal_ref, ahead_ref, arrived_ref, incoming_ref, behind_ref, dist_ref, high_ref, low_ref,
+                    out_sems, in_sems, back_out_sems, back_in_sems):
+    me = lax.axis_index("wide")
+    halves = (slots + 1) // 2
+    features = points_ref.shape[0]
+
+    def shift(step):
+        return devices // 2 + (step // 2) * (1 - 2 * (step % 2))
+
+    def computed(peer):
+        first = ((me < peer).astype(jnp.int32) + (me + peer) % 2) % 2
+        return slots // 2 + first * (halves - slots // 2)
+
+    def forward(peer, half):
+        return pltpu.make_async_remote_copy(
+            src_ref=outgoing_ref.at[peer * halves + half], dst_ref=incoming_ref.at[me * halves + half],
+            send_sem=out_sems.at[peer * halves + half], recv_sem=in_sems.at[me * halves + half],
+            device_id={"wide": peer}, device_id_type=MESH)
+
+    def forward_arrival(peer, half):
+        return pltpu.make_async_remote_copy(
+            src_ref=outgoing_ref.at[peer * halves + half], dst_ref=incoming_ref.at[peer * halves + half],
+            send_sem=out_sems.at[peer * halves + half], recv_sem=in_sems.at[peer * halves + half],
+            device_id={"wide": peer}, device_id_type=MESH)
+
+    def back(peer, half):
+        return pltpu.make_async_remote_copy(
+            src_ref=behind_ref.at[peer * halves + half], dst_ref=arrived_ref.at[me * halves + half],
+            send_sem=back_out_sems.at[peer * halves + half], recv_sem=back_in_sems.at[me * halves + half],
+            device_id={"wide": peer}, device_id_type=MESH)
+
+    def back_arrival(peer, half):
+        return pltpu.make_async_remote_copy(
+            src_ref=behind_ref.at[peer * halves + half], dst_ref=arrived_ref.at[peer * halves + half],
+            send_sem=back_out_sems.at[peer * halves + half], recv_sem=back_in_sems.at[peer * halves + half],
+            device_id={"wide": peer}, device_id_type=MESH)
+
+    def every(count_of, peer_of, action):
+        def visit(step, carry):
+            peer = peer_of(step)
+
+            def one(half, inner):
+                action(peer, half)
+                return inner
+
+            return lax.fori_loop(0, count_of(peer), one, carry)
+
+        lax.fori_loop(1, devices, visit, 0)
+
+    def target(step):
+        return (me + shift(step)) % devices
+
+    def source(step):
+        return (me + devices - shift(step)) % devices
+
+    greet(devices, me)
+    every(lambda peer: slots - computed(peer), target, lambda peer, half: forward(peer, half).start())
+
+    def diagonal_turn(block, carry):
         at = pl.ds(pl.multiple_of(block * size, size), size)
         own = points_ref[:, at]
-        shift = own - own[:, 0:1]
+        own = own - own[:, 0:1]
         _, product = tile_products(
-            inverse_ref, shift, shift, direction_ref[:, at], None, dist_ref, high_ref, low_ref, probes
+            inverse_ref, own, own, direction_ref[:, at], None, dist_ref, high_ref, low_ref, probes
         )
-        out_ref[:, at] = product
-        return carry
-
-    lax.fori_loop(0, points_ref.shape[1] // size, turn, 0)
+        diagonal_ref[:, at] = product
+        return carry
+
+    lax.fori_loop(0, points_ref.shape[1] // size, diagonal_turn, 0)
+
+    def cross_turn(peer, half):
+        item = peer * halves + half
+        forward_arrival(peer, half).wait_recv()
+        own = kept_ref[item, 0:features, :]
+        far = incoming_ref[item, 0:features, :]
+        weight = (me < peer).astype(jnp.float32)
+        anchor = weight * own[:, 0:1] + (1.0 - weight) * far[:, 0:1]
+        ahead, behind = tile_products(
+            inverse_ref, own - anchor, far - anchor, kept_ref[item, features:, :], incoming_ref[item, features:, :],
+            dist_ref, high_ref, low_ref, probes
+        )
+        ahead_ref[item] = ahead
+        behind_ref[item] = behind
+        back(peer, half).start()
+
+    every(computed, source, cross_turn)
+    every(lambda peer: slots - computed(peer), target, lambda peer, half: forward(peer, half).wait_send())
+    every(computed, source, lambda peer, half: back(peer, half).wait_send())
+    every(lambda peer: slots - computed(peer), target, lambda peer, half: back_arrival(peer, half).wait_recv())
 
 
 def tile_scratch(settings, size):
@@ -133,52 +222,64 @@
     ]
 
 
-def diagonal_products(inverse, points, direction, size):
+def exchange_products(devices, slots, inverse, points, direction, kept, outgoing, size):
     settings = inverse.shape[0]
-    return pl.pallas_call(
-        functools.partial(diagonal_kernel, size, direction.shape[0] // settings),
-        out_shape=jax.ShapeDtypeStruct(direction.shape, jnp.float32),
-        in_specs=[pl.BlockSpec(memory_space=SMEM)] + [pl.BlockSpec(memory_space=VMEM)] * 2,
-        out_specs=pl.BlockSpec(memory_space=VMEM),
-        scratch_shapes=tile_scratch(settings, size),
-        compiler_params=pltpu.CompilerParams(vmem_limit_bytes=VMEM_LIMIT),
-        cost_estimate=pl.CostEstimate(flops=40_000_000_000, bytes_accessed=6_000_000, transcendentals=0),
-    )(inverse, points, direction)
-
-
-def cross_kernel(size, probes, inverse_ref, index_ref, first_ref, points_ref, direction_ref, far_ref,
-                 ahead_ref, behind_ref, dist_ref, high_ref, low_ref):
-    item = pl.program_id(0)
-    features = points_ref.shape[0]
-    at = pl.ds(pl.multiple_of(index_ref[item] * size, size), size)
-    own = points_ref[:, at]
-    far = far_ref[0, 0:features, :]
-    anchor = jnp.where(first_ref[item] == 1, own[:, 0:1], far[:, 0:1])
-    ahead, behind = tile_products(
-        inverse_ref, own - anchor, far - anchor, direction_ref[:, at], far_ref[0, features:, :],
-        dist_ref, high_ref, low_ref, probes
-    )
-    ahead_ref[0] = ahead
-    behind_ref[0] = behind
-
-
-def cross_products(inverse, index, first, points, direction, far, size):
-    settings = inverse.shape[0]
-    items, rows = far.shape[:2]
+    items, rows = outgoing.shape[:2]
     columns = direction.shape[0]
     result = jax.ShapeDtypeStruct((items, columns, size), jnp.float32)
-    result_spec = pl.BlockSpec((1, columns, size), lambda i: (i, 0, 0))
     return pl.pallas_call(
-        functools.partial(cross_kernel, size, columns // settings),
-        grid=(items,),
-        out_shape=(result, result),
-        in_specs=[pl.BlockSpec(memory_space=SMEM)] * 3
-        + [pl.BlockSpec(memory_space=VMEM)] * 2
-        + [pl.BlockSpec((1, rows, size), lambda i: (i, 0, 0))],
-        out_specs=(result_spec, result_spec),
-        scratch_shapes=tile_scratch(settings, size),
-        compiler_params=pltpu.CompilerParams(vmem_limit_bytes=VMEM_LIMIT),
-    )(inverse, index, first, points, direction, far)
+        functools.partial(exchange_kernel, devices, slots, size, columns // settings),
+        out_shape=(jax.ShapeDtypeStruct(direction.shape, jnp.float32), result, result),
+        in_specs=[pl.BlockSpec(memory_space=SMEM)]
+        + [pl.BlockSpec(memory_space=VMEM)] * 3
+        + [pl.BlockSpec(memory_space=pl.ANY)],
+        out_specs=(pl.BlockSpec(memory_space=VMEM),) * 3,
+        scratch_shapes=[pltpu.VMEM((items, rows, size), jnp.float32), pltpu.VMEM((items, columns, size), jnp.float32)]
+        + tile_scratch(settings, size)
+        + [pltpu.SemaphoreType.DMA((items,))] * 4,
+        compiler_params=pltpu.CompilerParams(
+            vmem_limit_bytes=VMEM_LIMIT, collective_id=0, has_side_effects=True
+        ),
+    )(inverse, points, direction, kept, outgoing)
+
+
+def totals_kernel(devices, sums_ref, out_ref, held_ref, out_sems, in_sems):
+    me = lax.axis_index("wide")
+    greet(devices, me)
+
+    def copy(target, slot):
+        return pltpu.make_async_remote_copy(
+            src_ref=sums_ref, dst_ref=held_ref.at[slot], send_sem=out_sems.at[target], recv_sem=in_sems.at[slot],
+            device_id={"wide": target}, device_id_type=MESH)
+
+    def send(step, carry):
+        copy((me + step) % devices, me).start()
+        return carry
+
+    lax.fori_loop(1, devices, send, 0)
+    held_ref[me] = sums_ref[...]
+
+    def arrive(step, carry):
+        peer = (me + step) % devices
+        copy(peer, peer).wait()
+        return carry
+
+    lax.fori_loop(1, devices, arrive, 0)
+    out_ref[...] = lax.fori_loop(
+        1, devices, lambda peer, total: total + held_ref[peer], held_ref[0]
+    )
+
+
+def sum_over_devices(devices, sums):
+    return pl.pallas_call(
+        functools.partial(totals_kernel, devices),
+        out_shape=jax.ShapeDtypeStruct(sums.shape, jnp.float32),
+        in_specs=[pl.BlockSpec(memory_space=VMEM)],
+        out_specs=pl.BlockSpec(memory_space=VMEM),
+        scratch_shapes=[pltpu.VMEM((devices,) + sums.shape, jnp.float32)]
+        + [pltpu.SemaphoreType.DMA((devices,))] * 2,
+        compiler_params=pltpu.CompilerParams(collective_id=1, has_side_effects=True),
+    )(sums)
 
 
 def combine_kernel(size, probes, noise_ref, own_ref, own_live_ref, sent_ref, sent_live_ref, ahead_ref, arrived_ref,
@@ -210,8 +311,11 @@
 
     zero = jnp.zeros((direction_ref.shape[0], 128), jnp.float32)
     sums = lax.fori_loop(0, direction_ref.shape[1] // 128, total, (zero,) * 4)
+    lane = lax.broadcasted_iota(jnp.int32, zero.shape, 1)
+    packed = zero
     for index in range(4):
-        sums_ref[index] = sums[index]
+        packed = jnp.where(lane == index, jnp.sum(sums[index], axis=1, keepdims=True), packed)
+    sums_ref[...] = packed
 
 
 def combine(noise, own, own_live, sent, sent_live, ahead, arrived, diagonal, direction, residual, size):
@@ -220,7 +324,7 @@
         functools.partial(combine_kernel, size, columns // noise.shape[0]),
         out_shape=(
             jax.ShapeDtypeStruct(direction.shape, jnp.float32),
-            jax.ShapeDtypeStruct((4, columns, 128), jnp.float32),
+            jax.ShapeDtypeStruct((columns, 128), jnp.float32),
         ),
         in_specs=[pl.BlockSpec(memory_space=SMEM)] * 5 + [pl.BlockSpec(memory_space=VMEM)] * 5,
         out_specs=(pl.BlockSpec(memory_space=VMEM),) * 2,
@@ -248,8 +352,7 @@
 
     own, own_live = table(jnp.where(first, 0, 1))
     sent, sent_live = table(jnp.where(first, 1, 0))
-    lower = jnp.repeat((my_index < peers).astype(jnp.int32), halves)
-    return own, own_live, sent, sent_live, lower
+    return slots, own, own_live, sent, sent_live
 
 
 def on_device(points, solution, residual, direction, lengthscales, noise_variance, link_peer):
@@ -258,17 +361,14 @@
     size = points.shape[1] // link_peer.shape[1]
     probes = direction.shape[0] // lengthscales.shape[0]
     inverse = SCALE / lengthscales
-    own, own_live, sent, sent_live, lower = slot_tables(link_peer, my_index, devices)
-    outgoing = gather_blocks(sent, points, direction, size)
-    incoming = lax.all_to_all(outgoing, "wide", split_axis=0, concat_axis=0, tiled=True)
-    diagonal = diagonal_products(inverse, points, direction, size)
-    ahead, behind = cross_products(inverse, own, lower, points, direction, incoming, size)
-    arrived = lax.all_to_all(behind, "wide", split_axis=0, concat_axis=0, tiled=True)
+    slots, own, own_live, sent, sent_live = slot_tables(link_peer, my_index, devices)
+    outgoing, kept = gather_blocks(sent, own, points, direction, size)
+    diagonal, ahead, arrived = exchange_products(devices, slots, inverse, points, direction, kept, outgoing, size)
     image, sums = combine(
         noise_variance, own, own_live, sent, sent_live, ahead, arrived, diagonal, direction, residual, size
     )
-    totals = lax.psum(jnp.sum(sums, axis=2), "wide")
-    old_norm, curvature, mixed, square = totals[0], totals[1], totals[2], totals[3]
+    totals = sum_over_devices(devices, sums)
+    old_norm, curvature, mixed, square = totals[:, 0], totals[:, 1], totals[:, 2], totals[:, 3]
     step_size = old_norm / curvature
     new_norm = old_norm - 2.0 * step_size * mixed + step_size * step_size * square
     ratio = new_norm / old_norm

time: 525 us -> 220 us (0.42)
  Pallas kernels: 331 us -> 208 us
  waiting for transfers between devices: 113 us -> 0 us
  starting transfers between devices: 35.5 us -> 0 us
  blocking collectives: 33.9 us -> 0 us
    pallas_call x3, Pallas kernels: 323 us -> 200 us  [the longest x1 181 us: exchange_products(): pl.pallas_call(functools.partial(exchange_kernel, devices, slots, size, c...]
    all_to_all x2 -> x0, waiting for transfers between devices: 113 us -> none  [the longest x1 113 us: on_device(): lax.all_to_all(outgoing, 'wide', split_axis=0, concat_axis=0, tiled=True)]
    all_to_all x2 -> x0, starting transfers between devices: 35.5 us -> none  [the longest x1 28.1 us: on_device(): lax.all_to_all(behind, 'wide', split_axis=0, concat_axis=0, tiled=True)]
    psum x1 -> x0, blocking collectives: 33.9 us -> none  [on_device(): totals = lax.psum(jnp.sum(sums, axis=2), 'wide')]
  transfers between devices with their start and end apart: 2 -> 0, of which waited for: 1 -> 0; matrix products, arithmetic and copies ran while one was open for 0% -> 0% of each run, Pallas kernels for 10% -> 0%
where the time goes in v2:
time: 220 us; the launch traced here: 218 us
  Pallas kernels  208 us (95%)
  other arithmetic  8.02 us (4%)
    pallas_call x1, Pallas kernels, exchange_products(): pl.pallas_call(functools.partial(exchange_kernel, devices, slots, size, c...  181 us
    pallas_call x1, Pallas kernels, sum_over_devices(): pl.pallas_call(functools.partial(totals_kernel, devices), out_shape=jax.S...  11.3 us
    pallas_call x1, Pallas kernels, combine(): pl.pallas_call(functools.partial(combine_kernel, size, columns // noise.s...  8.15 us
    pallas_call x1, Pallas kernels, gather_blocks(): pl.pallas_call(functools.partial(gather_kernel, size), out_shape=(jax.Sha...  8.14 us

profile of v2, /device:TPU:0, one launch (start us, length us, event | category | flops | bytes accessed | tf_op | source)
XLA Modules:
  0.0 218.3 jit_solution(5097317829479720859)
XLA Ops:
  0.6 1.2 broadcast_divide_fusion.inverse_ref
  1.8 0.8 slice_bitcast_fusion.1
  2.6 0.1 select_reduce_fusion
  2.7 0.1 fusion.2
  2.8 0.1 and.38
  2.8 0.1 and.39
  2.9 0.1 multiply_add_fusion.2
  3.0 0.1 add.101
  3.1 0.1 add.97
  3.2 0.6 broadcast_select_fusion
  3.8 0.6 fusion.5
  4.3 8.1 %shard_map.94 = (f32[64,96,256]{2,1,0:T(8,128)}, f32[64,96,256]{2,1,0:T(8,128)}) custom-call(s32[64]{0:T(128)} %get-tuple-element.28.sent_ref, s32[64]{0:T(128)} %get-tuple-element.29.own_ref, f32[64,12288]{1,0:T(8,128)} %points_ref.3, f32[32,12288]{1,0:T(8,128)} %direction_ref.5), custom_call_target="tpu_custom_call" | custom-call | tf_op jit(solution)/shard_map/pallas_call | solution.py:105
  12.5 180.8 %shard_map.95 = (f32[32,12288]{1,0:T(8,128)}, f32[64,32,256]{2,1,0:T(8,128)}, f32[64,32,256]{2,1,0:T(8,128)}) custom-call(f32[4]{0:T(128)} %broadcast_divide_fusion.inverse_ref, f32[64,12288]{1,0:T(8,128)} %points_ref.3, f32[32,12288]{1,0:T(8,128)} %direction_ref.5, f32[64,96,256]{2,1,0:T(8,128)} %get-tuple-element.10.kept_ref, ...), custom_call_target="tpu_custom_call" | custom-call | tf_op jit(solution)/shard_map/pallas_call | solution.py:230
  193.3 0.0 copy-start
  193.3 0.0 copy-start.1
  193.3 8.1 %shard_map.96 = (f32[32,12288]{1,0:T(8,128)}, f32[32,128]{1,0:T(8,128)}) custom-call(f32[4]{0:T(128)} %noise_ref.1, s32[64]{0:T(128)} %get-tuple-element.29.own_ref, s32[64]{0:T(128)} %get-tuple-element.27.own_live_ref, s32[64]{0:T(128)} %get-tuple-element.28.sent_ref, s32[64]{0:T(128)} %get-tuple-element.26.sent_live_ref, ...), custom_call_target="tpu_custom_call" | custom-call | tf_op jit(solution)/shard_map/pallas_call | solution.py:323
  201.4 11.3 %shard_map.97 = f32[32,128]{1,0:T(8,128)} custom-call(f32[32,128]{1,0:T(8,128)} %get-tuple-element.15.sums_ref), custom_call_target="tpu_custom_call" | custom-call | tf_op jit(solution)/shard_map/pallas_call | solution.py:274
  212.8 1.1 fusion
  213.9 0.0 copy-done
  213.9 0.0 copy-done.1
  213.9 4.4 %multiply_add_fusion = (f32[32,12288]{1,0:T(8,128)}, f32[32,12288]{1,0:T(8,128)}, f32[32,12288]{1,0:T(8,128)}) fusion(f32[32,12288]{1,0:T(8,128)S(1)} %copy-done, f32[32]{0:T(128)S(1)} %get-tuple-element.17, f32[32,12288]{1,0:T(8,128)S(1)} %copy-done.1, f32[32,12288]{1,0:T(8,128)} %get-tuple-element.16, f32[32]{0:T(128)S(1)} %get-tuple-element.18, ...), kind=kLoop, calls=%fused_computation | loop fusion | flops 2359296 | bytes 11010304 | tf_op jit(solution)/shard_map/add | solution.py:377
  (2 shorter events, 0.0 us)
Async XLA Ops:
  193.3 20.6 %copy-start = (f32[32,12288]{1,0:T(8,128)S(1)}, f32[32,12288]{1,0:T(8,128)}, u32[]{:S(2)}) copy-start(f32[32,12288]{1,0:T(8,128)} %direction_ref.5) | copy-start | bytes 4718596
  193.3 20.6 %copy-start.1 = (f32[32,12288]{1,0:T(8,128)S(1)}, f32[32,12288]{1,0:T(8,128)}, u32[]{:S(2)}) copy-start(f32[32,12288]{1,0:T(8,128)} %residual_ref.1) | copy-start | bytes 4718596

commit v3 on v2

--- a/solution.py
+++ b/solution.py
@@ -90,9 +90,11 @@
 def gather_kernel(size, sent_ref, own_ref, points_ref, direction_ref, out_ref, kept_ref):
     features = points_ref.shape[0]
 
+    base = pl.program_id(0) * out_ref.shape[0]
+
     def copy(item, carry):
         for index_ref, result_ref in ((sent_ref, out_ref), (own_ref, kept_ref)):
-            block = pl.ds(pl.multiple_of(index_ref[item] * size, size), size)
+            block = pl.ds(pl.multiple_of(index_ref[base + item] * size, size), size)
             result_ref[item, 0:features, :] = points_ref[:, block]
             result_ref[item, features:, :] = direction_ref[:, block]
         return carry
@@ -102,11 +104,15 @@
 
 def gather_blocks(sent, own, points, direction, size):
     rows = points.shape[0] + direction.shape[0]
+    items = sent.shape[0]
+    group = 8 if items % 8 == 0 else 1
+    result_spec = pl.BlockSpec((group, rows, size), lambda i: (i, 0, 0))
     return pl.pallas_call(
         functools.partial(gather_kernel, size),
+        grid=(items // group,),
         out_shape=(jax.ShapeDtypeStruct((sent.shape[0], rows, size), jnp.float32),) * 2,
         in_specs=[pl.BlockSpec(memory_space=SMEM)] * 2 + [pl.BlockSpec(memory_space=VMEM)] * 2,
-        out_specs=(pl.BlockSpec(memory_space=VMEM),) * 2,
+        out_specs=(result_spec,) * 2,
         compiler_params=pltpu.CompilerParams(vmem_limit_bytes=VMEM_LIMIT),
     )(sent, own, points, direction)
 
@@ -122,15 +128,15 @@
     pl.semaphore_wait(barrier, devices - 1)
 
 
-def exchange_kernel(devices, slots, size, probes, inverse_ref, points_ref, direction_ref, kept_ref, outgoing_ref,
+def exchange_kernel(devices, slots, size, probes, inverse_ref, points_hbm, direction_hbm, kept_hbm, outgoing_ref,
                     diagonal_ref, ahead_ref, arrived_ref, incoming_ref, behind_ref, dist_ref, high_ref, low_ref,
-                    out_sems, in_sems, back_out_sems, back_in_sems):
+                    points_ref, direction_ref, kept_ref, local_sems, out_sems, in_sems, back_out_sems, back_in_sems):
     me = lax.axis_index("wide")
     halves = (slots + 1) // 2
     features = points_ref.shape[0]
 
     def shift(step):
-        return devices // 2 + (step // 2) * (1 - 2 * (step % 2))
+        return (step * (devices // 2 - 1)) % devices
 
     def computed(peer):
         first = ((me < peer).astype(jnp.int32) + (me + peer) % 2) % 2
@@ -180,6 +186,14 @@
 
     greet(devices, me)
     every(lambda peer: slots - computed(peer), target, lambda peer, half: forward(peer, half).start())
+    points_copy = pltpu.make_async_copy(points_hbm, points_ref, local_sems.at[0])
+    direction_copy = pltpu.make_async_copy(direction_hbm, direction_ref, local_sems.at[1])
+    kept_copy = pltpu.make_async_copy(kept_hbm, kept_ref, local_sems.at[2])
+    points_copy.start()
+    direction_copy.start()
+    kept_copy.start()
+    points_copy.wait()
+    direction_copy.wait()
 
     def diagonal_turn(block, carry):
         at = pl.ds(pl.multiple_of(block * size, size), size)
@@ -192,6 +206,7 @@
         return carry
 
     lax.fori_loop(0, points_ref.shape[1] // size, diagonal_turn, 0)
+    kept_copy.wait()
 
     def cross_turn(peer, half):
         item = peer * halves + half
@@ -230,12 +245,12 @@
     return pl.pallas_call(
         functools.partial(exchange_kernel, devices, slots, size, columns // settings),
         out_shape=(jax.ShapeDtypeStruct(direction.shape, jnp.float32), result, result),
-        in_specs=[pl.BlockSpec(memory_space=SMEM)]
-        + [pl.BlockSpec(memory_space=VMEM)] * 3
-        + [pl.BlockSpec(memory_space=pl.ANY)],
+        in_specs=[pl.BlockSpec(memory_space=SMEM)] + [pl.BlockSpec(memory_space=pl.ANY)] * 4,
         out_specs=(pl.BlockSpec(memory_space=VMEM),) * 3,
         scratch_shapes=[pltpu.VMEM((items, rows, size), jnp.float32), pltpu.VMEM((items, columns, size), jnp.float32)]
         + tile_scratch(settings, size)
+        + [pltpu.VMEM(array.shape, jnp.float32) for array in (points, direction, kept)]
+        + [pltpu.SemaphoreType.DMA((3,))]
         + [pltpu.SemaphoreType.DMA((items,))] * 4,
         compiler_params=pltpu.CompilerParams(
             vmem_limit_bytes=VMEM_LIMIT, collective_id=0, has_side_effects=True

time: 220 us -> 207 us (0.941)
  Pallas kernels: 208 us -> 196 us
    pallas_call x1, Pallas kernels: 181 us -> 170 us  [exchange_products(): pl.pallas_call(functools.partial(exchange_kernel, devices, slots, size, c...]
where the time goes in v3:
time: 207 us; the launch traced here: 206 us
  Pallas kernels  196 us (95%)
  other arithmetic  8.02 us (4%)
    pallas_call x1, Pallas kernels, exchange_products(): pl.pallas_call(functools.partial(exchange_kernel, devices, slots, size, c...  170 us
    pallas_call x1, Pallas kernels, sum_over_devices(): pl.pallas_call(functools.partial(totals_kernel, devices), out_shape=jax.S...  9.18 us
    pallas_call x1, Pallas kernels, gather_blocks(): pl.pallas_call(functools.partial(gather_kernel, size), grid=(items // gro...  8.26 us
    pallas_call x1, Pallas kernels, combine(): pl.pallas_call(functools.partial(combine_kernel, size, columns // noise.s...  8.15 us
    add x1, other arithmetic, on_device(): new_direction = new_residual + ratio[:, None] * direction  4.39 us

profile of v3, /device:TPU:0, one launch (start us, length us, event | category | flops | bytes accessed | tf_op | source)
XLA Modules:
  0.0 205.9 jit_solution(83736583606642335)
XLA Ops:
  0.6 1.2 broadcast_divide_fusion.inverse_ref
  1.8 0.8 slice_bitcast_fusion.1
  2.6 0.1 select_reduce_fusion
  2.7 0.1 fusion.2
  2.8 0.1 and.38
  2.8 0.1 and.39
  2.9 0.1 multiply_add_fusion.2
  3.0 0.1 add.101
  3.1 0.1 add.97
  3.2 0.6 broadcast_select_fusion
  3.8 0.6 fusion.5
  4.3 8.3 %shard_map.94 = (f32[64,96,256]{2,1,0:T(8,128)}, f32[64,96,256]{2,1,0:T(8,128)}) custom-call(s32[64]{0:T(128)} %get-tuple-element.28.sent_ref, s32[64]{0:T(128)} %get-tuple-element.29.own_ref, f32[64,12288]{1,0:T(8,128)} %points_hbm.1, f32[32,12288]{1,0:T(8,128)} %direction_ref.3), custom_call_target="tpu_custom_call" | custom-call | tf_op jit(solution)/shard_map/pallas_call | solution.py:110
  12.6 170.5 %shard_map.95 = (f32[32,12288]{1,0:T(8,128)}, f32[64,32,256]{2,1,0:T(8,128)}, f32[64,32,256]{2,1,0:T(8,128)}) custom-call(f32[4]{0:T(128)} %broadcast_divide_fusion.inverse_ref, f32[64,12288]{1,0:T(8,128)} %points_hbm.1, f32[32,12288]{1,0:T(8,128)} %direction_ref.3, f32[64,96,256]{2,1,0:T(8,128)} %get-tuple-element.10.kept_hbm, ...), custom_call_target="tpu_custom_call" | custom-call | tf_op jit(solution)/shard_map/pallas_call | solution.py:245
  183.1 0.0 copy-start
  183.1 0.0 copy-start.1
  183.1 8.1 %shard_map.96 = (f32[32,12288]{1,0:T(8,128)}, f32[32,128]{1,0:T(8,128)}) custom-call(f32[4]{0:T(128)} %noise_ref.1, s32[64]{0:T(128)} %get-tuple-element.29.own_ref, s32[64]{0:T(128)} %get-tuple-element.27.own_live_ref, s32[64]{0:T(128)} %get-tuple-element.28.sent_ref, s32[64]{0:T(128)} %get-tuple-element.26.sent_live_ref, ...), custom_call_target="tpu_custom_call" | custom-call | tf_op jit(solution)/shard_map/pallas_call | solution.py:338
  191.3 9.2 %shard_map.97 = f32[32,128]{1,0:T(8,128)} custom-call(f32[32,128]{1,0:T(8,128)} %get-tuple-element.15.sums_ref), custom_call_target="tpu_custom_call" | custom-call | tf_op jit(solution)/shard_map/pallas_call | solution.py:289
  200.5 1.1 fusion
  201.5 0.0 copy-done
  201.5 0.0 copy-done.1
  201.5 4.4 %multiply_add_fusion = (f32[32,12288]{1,0:T(8,128)}, f32[32,12288]{1,0:T(8,128)}, f32[32,12288]{1,0:T(8,128)}) fusion(f32[32,12288]{1,0:T(8,128)S(1)} %copy-done, f32[32]{0:T(128)S(1)} %get-tuple-element.17, f32[32,12288]{1,0:T(8,128)S(1)} %copy-done.1, f32[32,12288]{1,0:T(8,128)} %get-tuple-element.16, f32[32]{0:T(128)S(1)} %get-tuple-element.18, ...), kind=kLoop, calls=%fused_computation | loop fusion | flops 2359296 | bytes 11010304 | tf_op jit(solution)/shard_map/add | solution.py:392
  (2 shorter events, 0.0 us)
Async XLA Ops:
  183.1 18.4 %copy-start = (f32[32,12288]{1,0:T(8,128)S(1)}, f32[32,12288]{1,0:T(8,128)}, u32[]{:S(2)}) copy-start(f32[32,12288]{1,0:T(8,128)} %direction_ref.3) | copy-start | bytes 4718596
  183.1 18.4 %copy-start.1 = (f32[32,12288]{1,0:T(8,128)S(1)}, f32[32,12288]{1,0:T(8,128)}, u32[]{:S(2)}) copy-start(f32[32,12288]{1,0:T(8,128)} %residual_ref.1) | copy-start | bytes 4718596

commit v4 on v3

--- a/solution.py
+++ b/solution.py
@@ -297,12 +297,20 @@
     )(sums)
 
 
-def combine_kernel(size, probes, noise_ref, own_ref, own_live_ref, sent_ref, sent_live_ref, ahead_ref, arrived_ref,
-                   diagonal_ref, direction_ref, residual_ref, image_ref, sums_ref):
+def combine_kernel(size, probes, noise_ref, own_ref, own_live_ref, sent_ref, sent_live_ref, ahead_hbm, arrived_hbm,
+                   residual_hbm, diagonal_ref, direction_ref, image_ref, sums_ref, ahead_ref, arrived_ref,
+                   residual_ref, sems):
+    pairs = ((ahead_hbm, ahead_ref), (arrived_hbm, arrived_ref), (residual_hbm, residual_ref))
+    copies = [pltpu.make_async_copy(pair[0], pair[1], sems.at[i]) for i, pair in enumerate(pairs)]
+    for copy in copies:
+        copy.start()
     settings = noise_ref.shape[0]
     for setting in range(settings):
         rows = pl.ds(setting * probes, probes)
         image_ref[rows, :] = diagonal_ref[rows, :] + noise_ref[setting] * direction_ref[rows, :]
+
+    copies[0].wait()
+    copies[1].wait()
 
     def add(item, carry):
         @pl.when(own_live_ref[item] == 1)
@@ -318,6 +326,7 @@
         return carry
 
     lax.fori_loop(0, ahead_ref.shape[0], add, 0)
+    copies[2].wait()
 
     def total(chunk, sums):
         at = pl.ds(pl.multiple_of(chunk * 128, 128), 128)
@@ -325,7 +334,7 @@
         return (sums[0] + r * r, sums[1] + d * m, sums[2] + r * m, sums[3] + m * m)
 
     zero = jnp.zeros((direction_ref.shape[0], 128), jnp.float32)
-    sums = lax.fori_loop(0, direction_ref.shape[1] // 128, total, (zero,) * 4)
+    sums = lax.fori_loop(0, direction_ref.shape[1] // 128, total, (zero,) * 4, unroll=2)
     lane = lax.broadcasted_iota(jnp.int32, zero.shape, 1)
     packed = zero
     for index in range(4):
@@ -341,10 +350,14 @@
             jax.ShapeDtypeStruct(direction.shape, jnp.float32),
             jax.ShapeDtypeStruct((columns, 128), jnp.float32),
         ),
-        in_specs=[pl.BlockSpec(memory_space=SMEM)] * 5 + [pl.BlockSpec(memory_space=VMEM)] * 5,
+        in_specs=[pl.BlockSpec(memory_space=SMEM)] * 5
+        + [pl.BlockSpec(memory_space=pl.ANY)] * 3
+        + [pl.BlockSpec(memory_space=VMEM)] * 2,
         out_specs=(pl.BlockSpec(memory_space=VMEM),) * 2,
+        scratch_shapes=[pltpu.VMEM(array.shape, jnp.float32) for array in (ahead, arrived, residual)]
+        + [pltpu.SemaphoreType.DMA((3,))],
         compiler_params=pltpu.CompilerParams(vmem_limit_bytes=VMEM_LIMIT),
-    )(noise, own, own_live, sent, sent_live, ahead, arrived, diagonal, direction, residual)
+    )(noise, own, own_live, sent, sent_live, ahead, arrived, residual, diagonal, direction)
 
 
 def slot_tables(link_peer, my_index, devices):

time: 207 us -> 207 us (level)
  no operation moved by 1% of the time
where the time goes in v4:
time: 207 us; the launch traced here: 206 us
  Pallas kernels  196 us (95%)
  other arithmetic  8.02 us (4%)
    pallas_call x1, Pallas kernels, exchange_products(): pl.pallas_call(functools.partial(exchange_kernel, devices, slots, size, c...  170 us
    pallas_call x1, Pallas kernels, sum_over_devices(): pl.pallas_call(functools.partial(totals_kernel, devices), out_shape=jax.S...  9.19 us
    pallas_call x1, Pallas kernels, gather_blocks(): pl.pallas_call(functools.partial(gather_kernel, size), grid=(items // gro...  8.26 us
    pallas_call x1, Pallas kernels, combine(): pl.pallas_call(functools.partial(combine_kernel, size, columns // noise.s...  8.08 us
    add x1, other arithmetic, on_device(): new_direction = new_residual + ratio[:, None] * direction  4.39 us

profile of v4, /device:TPU:0, one launch (start us, length us, event | category | flops | bytes accessed | tf_op | source)
XLA Modules:
  0.0 205.9 jit_solution(8873611785811855063)
XLA Ops:
  0.6 1.2 broadcast_divide_fusion.inverse_ref
  1.8 0.8 slice_bitcast_fusion.1
  2.6 0.1 select_reduce_fusion
  2.7 0.1 fusion.2
  2.8 0.1 and.38
  2.8 0.1 and.39
  2.9 0.1 multiply_add_fusion.2
  3.0 0.1 add.101
  3.1 0.1 add.97
  3.2 0.6 broadcast_select_fusion
  3.8 0.6 fusion.5
  4.3 8.3 %shard_map.94 = (f32[64,96,256]{2,1,0:T(8,128)}, f32[64,96,256]{2,1,0:T(8,128)}) custom-call(s32[64]{0:T(128)} %get-tuple-element.28.sent_ref, s32[64]{0:T(128)} %get-tuple-element.29.own_ref, f32[64,12288]{1,0:T(8,128)} %points_hbm.1, f32[32,12288]{1,0:T(8,128)} %direction_ref.3), custom_call_target="tpu_custom_call" | custom-call | tf_op jit(solution)/shard_map/pallas_call | solution.py:110
  12.6 170.5 %shard_map.95 = (f32[32,12288]{1,0:T(8,128)}, f32[64,32,256]{2,1,0:T(8,128)}, f32[64,32,256]{2,1,0:T(8,128)}) custom-call(f32[4]{0:T(128)} %broadcast_divide_fusion.inverse_ref, f32[64,12288]{1,0:T(8,128)} %points_hbm.1, f32[32,12288]{1,0:T(8,128)} %direction_ref.3, f32[64,96,256]{2,1,0:T(8,128)} %get-tuple-element.10.kept_hbm, ...), custom_call_target="tpu_custom_call" | custom-call | tf_op jit(solution)/shard_map/pallas_call | solution.py:245
  183.1 0.0 copy-start
  183.1 0.0 copy-start.1
  183.1 8.1 %shard_map.96 = (f32[32,12288]{1,0:T(8,128)}, f32[32,128]{1,0:T(8,128)}) custom-call(f32[4]{0:T(128)} %noise_ref.1, s32[64]{0:T(128)} %get-tuple-element.29.own_ref, s32[64]{0:T(128)} %get-tuple-element.27.own_live_ref, s32[64]{0:T(128)} %get-tuple-element.28.sent_ref, s32[64]{0:T(128)} %get-tuple-element.26.sent_live_ref, ...), custom_call_target="tpu_custom_call" | custom-call | tf_op jit(solution)/shard_map/pallas_call | solution.py:347
  191.2 9.2 %shard_map.97 = f32[32,128]{1,0:T(8,128)} custom-call(f32[32,128]{1,0:T(8,128)} %get-tuple-element.15.sums_ref), custom_call_target="tpu_custom_call" | custom-call | tf_op jit(solution)/shard_map/pallas_call | solution.py:289
  200.4 1.1 fusion
  201.5 0.0 copy-done
  201.5 0.0 copy-done.1
  201.5 4.4 %multiply_add_fusion = (f32[32,12288]{1,0:T(8,128)}, f32[32,12288]{1,0:T(8,128)}, f32[32,12288]{1,0:T(8,128)}) fusion(f32[32,12288]{1,0:T(8,128)S(1)} %copy-done, f32[32]{0:T(128)S(1)} %get-tuple-element.17, f32[32,12288]{1,0:T(8,128)S(1)} %copy-done.1, f32[32,12288]{1,0:T(8,128)} %get-tuple-element.16, f32[32]{0:T(128)S(1)} %get-tuple-element.18, ...), kind=kLoop, calls=%fused_computation | loop fusion | flops 2359296 | bytes 11010304 | tf_op jit(solution)/shard_map/add | solution.py:405
  (2 shorter events, 0.0 us)
Async XLA Ops:
  183.1 18.4 %copy-start = (f32[32,12288]{1,0:T(8,128)S(1)}, f32[32,12288]{1,0:T(8,128)}, u32[]{:S(2)}) copy-start(f32[32,12288]{1,0:T(8,128)} %direction_ref.3) | copy-start | bytes 4718596
  183.1 18.4 %copy-start.1 = (f32[32,12288]{1,0:T(8,128)S(1)}, f32[32,12288]{1,0:T(8,128)}, u32[]{:S(2)}) copy-start(f32[32,12288]{1,0:T(8,128)} %residual_hbm.1) | copy-start | bytes 4718596
